TPU v7x, 32 devices: a whole 2x2x4 slice. The times are simulated.
32 devices in a mesh: parts: 2 (over y), pair: 4 (over z), aux: 2 (over x), occ: 2 (over core).
Axes of the slice: x: 2, y: 2, z: 4, core: 2. Of those that a mesh axis runs over, the one named last changes fastest.
Arguments:
- three_index: bfloat16 [64, 128, 16, 128], P(('parts', 'pair'), 'aux'), parts along dimension 0, may hold values from -0.5 to 0.5
- coefficients: bfloat16 [1024, 1024], P(('parts', 'pair'), 'occ'), parts along dimension 0, may hold values from -6 to 6
- shell_size: int32 [64], P(('parts', 'pair')), parts along dimension 0, may hold values from 1 to 10
- ket_shell: int32 [64, 8], P(('parts', 'pair')), parts along dimension 0, may hold values from 0 to 31
- ket_count: int32 [64], P(('parts', 'pair')), parts along dimension 0, may hold values from 1 to 8
Outputs:
- exchange_k: float32 [1024, 384], P(('parts', 'pair', 'aux', 'occ')), parts along dimension 0
There are 2 independent parts, one for each index of `parts`. A program takes and returns all parts, laid end to end along the dimension named above; each array names one. Nothing has to cross between parts.
All inputs are finite; a program needn't handle non-finite values.
Results may differ from a plain program's by a relative error of at most 0.0003.
Values may be sent and summed in bfloat16 or wider, within the bound.
A program may use at most 64 MiB of HBM per device.

v0:
```python
import math

import jax
import jax.numpy as jnp
from jax import lax
from jax.sharding import PartitionSpec as P


def passed_along(x, axis, by):
    devices = lax.axis_size(axis)
    pairs = [(i, i + by) for i in range(devices) if 0 <= i + by < devices]
    return lax.ppermute(x, axis, pairs)


def shards(three_index, coefficients, shell_size, ket_shell, ket_count):
    shells, aux_rows, width, span = three_index.shape
    slots = span // width
    lanes = jnp.arange(width, dtype=jnp.int32)
    shell_mask = lanes[None, :] < shell_size[:, None]
    coef_masked = jnp.where(
        shell_mask.reshape(shells * width)[:, None], coefficients, jnp.zeros_like(coefficients)
    )
    whole = lax.all_gather(coef_masked, "pair", axis=0, tiled=True)
    orbitals = whole.shape[1]
    total_aux = aux_rows * lax.axis_size("aux")
    total_occ = orbitals * lax.axis_size("occ")
    scale = 1.0 / math.sqrt(total_aux * total_occ)
    slot_ids = jnp.arange(slots, dtype=jnp.int32)
    functions = shells * width

    def one_shell(packed):
        kets, count, block, mask = packed
        index = (kets[:, None] * width + lanes[None, :]).reshape(slots * width)
        rows = whole[index]
        live = jnp.repeat(slot_ids < count, width)
        rows = jnp.where(live[:, None], rows, jnp.zeros_like(rows))
        product = jnp.dot(
            block.reshape(aux_rows * width, span), rows, preferred_element_type=jnp.float32
        )
        product = (
            product.reshape(aux_rows, width, orbitals) * mask.astype(jnp.float32)[None, :, None]
        )
        return product.astype(jnp.bfloat16)

    half = lax.map(one_shell, (ket_shell, ket_count, three_index, shell_mask))
    next_part = passed_along(half, "pair", -1)
    own_tile = jnp.einsum("bpfi,cpgi->bfcg", half, half, preferred_element_type=jnp.float32)
    own_tile = own_tile.reshape(functions, functions) * scale
    right_tile = jnp.einsum("bpfi,cpgi->bfcg", half, next_part, preferred_element_type=jnp.float32)
    right_tile = right_tile.reshape(functions, functions) * scale
    left_tile = passed_along(right_tile.T.astype(jnp.bfloat16), "pair", 1).astype(jnp.float32)
    tiles = jnp.concatenate([left_tile, own_tile, right_tile], axis=1)
    return lax.psum_scatter(tiles, ("aux", "occ"), scatter_dimension=0, tiled=True)


def solution(mesh):
    return jax.shard_map(
        shards,
        mesh=mesh,
        in_specs=(
            P(("parts", "pair"), "aux", None, None),
            P(("parts", "pair"), "occ"),
            P(("parts", "pair")),
            P(("parts", "pair"), None),
            P(("parts", "pair")),
        ),
        out_specs=P(("parts", "pair", "aux", "occ"), None),
        check_vma=False,
    )
```

profile of v0, /device:TPU:0, one launch (start us, length us, event | category | flops | bytes accessed | tf_op | source)
XLA Modules:
  0.0 311.8 jit_solution(2137067301563984607)
XLA Ops:
  6.5 0.7 iota_compare_fusion.1
  7.4 1.0 broadcast_select_fusion
  8.4 17.4 %all_gather.3 = bf16[512,512]{1,0:T(8,128)(2,1)S(1)} all-gather(bf16[128,512]{1,0:T(8,128)(2,1)S(1)} %broadcast_select_fusion), channel_id=1, replica_groups=mesh['parts'=2,'pair'=4,'aux'=2,'occ'=2] {'pair'}, dimensions={0}, use_global_device_ids=true | all-gather | bytes 655360 | tf_op jit(solution)/shard_map/all_gather | solution.py:23
  25.7 48.8 %while.11 = (s32[]{:T(128)}, bf16[8,64,16,512]{3,2,1,0:T(8,128)(2,1)}, bf16[8,64,16,128]{3,2,1,0:T(8,128)(2,1)}, s32[8]{0:T(128)}, s32[8,8]{1,0:T(8,128)}, /*ind...) while((s32[]{:T(128)}, bf16[8,64,16,512]{3,2,1,0:T(8,128)(2,1)}, ...), condition=%wide.region_1.2_spmd.clone, body=%wide.region_0.1_spmd.clone.sunk | while | flops 135333408 | bytes 1713517 | solution.py:45
  25.7 0.7 fusion.53
  26.6 0.8 gather_fusion
  27.4 1.2 dynamic_slice.39
  28.6 0.5 iota_compare_fusion.3
  29.4 2.4 fusion.55
  31.8 0.7 fusion.53
  32.6 0.8 gather_fusion
  33.5 1.2 dynamic_slice.39
  34.7 0.5 iota_compare_fusion.3
  35.4 2.5 fusion.55
  37.9 0.7 fusion.53
  38.8 0.8 gather_fusion
  39.6 1.2 dynamic_slice.39
  40.8 0.5 iota_compare_fusion.3
  41.6 2.4 fusion.55
  44.0 0.7 fusion.53
  44.9 0.8 gather_fusion
  45.7 1.2 dynamic_slice.39
  46.9 0.5 iota_compare_fusion.3
  47.6 2.4 fusion.55
  50.1 0.7 fusion.53
  50.9 0.8 gather_fusion
  51.8 1.2 dynamic_slice.39
  53.7 2.4 fusion.55
  56.2 0.7 fusion.53
  57.0 0.8 gather_fusion
  57.9 1.2 dynamic_slice.39
  59.1 0.5 iota_compare_fusion.3
  59.8 2.4 fusion.55
  62.3 0.7 fusion.53
  63.1 0.8 gather_fusion
  64.0 1.2 dynamic_slice.39
  65.9 2.5 fusion.55
  68.4 0.7 fusion.53
  69.2 0.8 gather_fusion
  70.1 1.2 dynamic_slice.39
  72.0 2.4 fusion.55
  74.5 1.3 collective-permute-start
  75.8 181.6 %collective-permute-done = bf16[8,64,16,512]{3,2,1,0:T(8,128)(2,1)S(1)} collective-permute-done((bf16[8,64,16,512]{3,2,1,0:T(8,128)(2,1)}, bf16[8,64,16,512]{3,2,1,0:T(8,128)(2,1)S(1)}, u32[]{:S(2)}, u32[]{:S(2)}) %collective-permute-start) | collective-permute-done | bytes 8388640 | tf_op jit(solution)/shard_map/ppermute | solution.py:12
  257.3 12.3 %fusion.29 = f32[8,16,8,16]{3,1,2,0:T(8,128)S(1)} fusion(bf16[8,64,16,512]{3,2,1,0:T(8,128)(2,1)S(1)} %collective-permute-done, bf16[8,64,16,512]{3,2,1,0:T(8,128)(2,1)} %get-tuple-element.52), kind=kOutput, calls=%fused_computation.31 | convolution fusion | flops 1073758208 | bytes 16842752 | tf_op jit(solution)/shard_map/bpfi,cpgi->bfcg/dot_general | solution.py:49
  270.1 1.7 collective-permute-start.1
  271.8 12.8 %fusion.39 = f32[8,16,8,16]{3,1,2,0:T(8,128)S(1)} fusion(bf16[8,64,16,512]{3,2,1,0:T(8,128)(2,1)} %get-tuple-element.52), kind=kOutput, calls=%fused_computation.33 | convolution fusion | flops 1073758208 | bytes 8454144 | tf_op jit(solution)/shard_map/bpfi,cpgi->bfcg/dot_general | solution.py:47
  285.0 0.7 pad_maximum_fusion
  285.7 19.3 %reduce-scatter.2.cloned.1.call-done = f32[32,384]{1,0:T(8,128)} async-done(((f32[128,384]{1,0:T(8,128)}), f32[32,384]{1,0:T(8,128)}) %reduce-scatter.2.cloned.1.call-update) | async-done | bytes 49168 | tf_op jit(solution)/shard_map/reduce_scatter | solution.py:53
  (70 shorter events, 5.3 us)
Async XLA Ops:
  6.5 298.4 %reduce-scatter.2.cloned.1.call-start = ((), (), s32[]{:S(2)}) async-start(), calls=%async_computation.1 | async-start | bytes 245760 | tf_op jit(solution)/shard_map/reduce_scatter | solution.py:53
  74.5 182.8 %collective-permute-start = (bf16[8,64,16,512]{3,2,1,0:T(8,128)(2,1)}, bf16[8,64,16,512]{3,2,1,0:T(8,128)(2,1)S(1)}, u32[]{:S(2)}, u32[]{:S(2)}) collective-permute-start(bf16[8,64,16,512]{3,2,1,0:T(8,128)(2,1)} %get-tuple-element.52), channel_id=1, source_target_pairs={{4,0},{8,4},{12,8},{5,1},{9,5},{13,9},{6,2},{10,6},{14,10},{7,3},{... | collective-permute-start | bytes 25165832 | tf_op jit(solution)/shard_map/ppermute | solution.py:12
  270.1 14.8 %collective-permute-start.1 = (bf16[128,128]{1,0:T(8,128)(2,1)S(1)}, bf16[128,128]{1,0:T(8,128)(2,1)S(1)}, u32[]{:S(2)}, u32[]{:S(2)}) collective-permute-start(bf16[128,128]{1,0:T(8,128)(2,1)S(1)} %bitcast.76), channel_id=1, source_target_pairs={{0,4},{4,8},{8,12},{1,5},{5,9},{9,13},{2,6},{6,10},{10,14},{3,7},{... | collective-permute-start | bytes 98312 | tf_op jit(solution)/shard_map/ppermute | solution.py:12
Sparse Core Ops, SparseCore 0:
  285.8 19.0 reduce-scatter.1
where the time goes:
time: 313 us; the launch traced here: 312 us
  waiting for transfers between devices  201 us (64%)
  matrix products  44.6 us (14%)
  local copies, waits for them, and re-layouts  19.3 us (6%)
  blocking collectives  17.4 us (6%)
  between operations  13.5 us (4%)
  other arithmetic  13.1 us (4%)
    ppermute x2, waiting for transfers between devices, passed_along(): return lax.ppermute(x, axis, pairs)  182 us
    dot_general x8, matrix products, one_shell(): jnp.dot(block.reshape(aux_rows * width, span), rows, preferred_element_ty...  19.5 us
    reduce_scatter x1, waiting for transfers between devices, shards(): lax.psum_scatter(tiles, ('aux', 'occ'), scatter_dimension=0, tiled=True)  19.3 us
    all_gather x1, blocking collectives, shards(): whole = lax.all_gather(coef_masked, 'pair', axis=0, tiled=True)  17.4 us
    dot_general x1, matrix products, shards(): jnp.einsum('bpfi,cpgi->bfcg', half, half, preferred_element_type=jnp.floa...  12.8 us
    dot_general x1, matrix products, shards(): jnp.einsum('bpfi,cpgi->bfcg', half, next_part, preferred_element_type=jnp...  12.3 us
    dynamic_slice x8, local copies, waits for them, and re-layouts, shards(): half = lax.map(one_shell, (ket_shell, ket_count, three_index, shell_mask))  9.68 us
    gather x8, local copies, waits for them, and re-layouts, one_shell(): rows = whole[index]  6.8 us
  transfers between devices with their start and end apart: 3, of which 2 were waited for; matrix products, arithmetic and copies ran while one was open for 4% of the time, Pallas kernels for 0%

commit v1 on v0

v1 whole, which is shorter than its diff:
```python
import functools
import math

import jax
import jax.numpy as jnp
from jax import lax
from jax.experimental import pallas as pl
from jax.experimental.pallas import tpu as pltpu
from jax.sharding import PartitionSpec as P

MESH = pl.DeviceIdType.MESH
NT = (((1,), (1,)), ((), ()))


def kernel(sizes, t_hbm, coef, size, ket, cnt, out, t_own, t_nb, coefs, pick, weights, half, half_nb, info,
           info_in, info_s, tiles, flips, red_same, red_cross, local_sem, coef_send, coef_fwd, coef_recv,
           info_send, info_recv, t_send, t_fwd, t_recv, same_send, same_recv, cross_send, cross_recv):
    n_pair, n_aux, n_occ, width, slots, chunks = sizes
    shells, rows, span = t_own.shape
    orbitals = coef.shape[1]
    functions = shells * width
    n_red = n_aux * n_occ
    share = shells // n_occ
    half_rows = rows // 2
    step = half_rows // chunks
    piece = functions // n_aux
    out_rows = functions // n_red
    nbas = n_pair * functions
    z = lax.axis_index("pair")
    x = lax.axis_index("aux")
    c = lax.axis_index("occ")
    mine = x * n_occ + c
    has_up = z + 1 < n_pair
    has_down = z > 0
    sides = ((has_up, 1), (has_down, -1))
    pending = []

    def when(cond, make, act):
        if cond is None:
            act(make())
        else:
            @pl.when(cond)
            def _():
                act(make())

    def begin(make, cond=None):
        when(cond, make, lambda d: d.start())
        pending.append((cond, make))

    def arrive(make, cond=None):
        when(cond, make, lambda d: d.wait_recv())

    def remote(src, dst, s_sem, r_sem, **where):
        return lambda: pltpu.make_async_remote_copy(
            src_ref=src(), dst_ref=dst(), send_sem=s_sem(), recv_sem=r_sem(),
            device_id={k: v() for k, v in where.items()}, device_id_type=MESH)

    local = pltpu.make_async_copy(t_hbm, t_own, local_sem.at[0])
    local.start()

    barrier = pltpu.get_barrier_semaphore()
    for delta in range(n_red):
        other = lax.rem(mine + delta, n_red)
        ox, oc = other // n_occ, lax.rem(other, n_occ)
        if delta > 0:
            pl.semaphore_signal(barrier, inc=1, device_id={"aux": ox, "occ": oc}, device_id_type=MESH)
        for has, way in sides:
            @pl.when(has)
            def _():
                pl.semaphore_signal(
                    barrier, inc=1, device_id={"pair": z + way, "aux": ox, "occ": oc}, device_id_type=MESH)

    first = pl.multiple_of(z * functions, functions)
    fun = lax.broadcasted_iota(jnp.int32, (width, orbitals), 0)
    for b in range(shells):
        block = coef[b * width:(b + 1) * width, :].astype(jnp.float32)
        block = jnp.where(fun < size[b], block, 0.0).astype(jnp.bfloat16)
        coefs[pl.ds(pl.multiple_of(first + b * width, width), width), :] = block

    row = lax.broadcasted_iota(jnp.int32, info.shape, 0)
    lane = lax.broadcasted_iota(jnp.int32, info.shape, 1)
    packed = jnp.zeros(info.shape, jnp.int32)
    for b in range(shells):
        line = jnp.where(lane == slots, cnt[b], jnp.where(lane == slots + 1, size[b], 0))
        for s in range(slots):
            line = jnp.where(lane == s, ket[b, s], line)
        packed = jnp.where(row == b, line, packed)
    info[...] = packed

    ups, downs = has_up.astype(jnp.int32), has_down.astype(jnp.int32)
    pl.semaphore_wait(barrier, n_red - 1 + n_red * (ups + downs))

    def part(owner, who):
        at = pl.multiple_of(owner * functions + who * piece, piece)
        return coefs.at[pl.ds(at, piece), :]

    def hop(owner, way, s):
        k = 0 if way > 0 else 1
        return remote(lambda: part(owner, x), lambda: part(owner, x), lambda: coef_send.at[k, s],
                      lambda: coef_recv.at[k, s, 0], pair=lambda: z + way)

    def across(owner, k, s, delta):
        return remote(lambda: part(owner, x), lambda: part(owner, x), lambda: coef_fwd.at[k, s, delta],
                      lambda: coef_recv.at[k, s, delta], aux=lambda: lax.rem(x + delta, n_aux))

    def across_in(owner, k, s, delta):
        who = lax.rem(x - delta + n_aux, n_aux)
        return remote(lambda: part(owner, who), lambda: part(owner, who), lambda: coef_fwd.at[k, s, delta],
                      lambda: coef_recv.at[k, s, delta], aux=lambda: lax.rem(x + delta, n_aux))

    def t_part(ref, lead, side, who, j):
        at = side * half_rows + j * step
        return ref.at[pl.ds(who * share, share), pl.ds(at, step), :]

    def t_hop(k, j):
        way = 1 if k == 0 else -1
        side = 1 if k == 0 else 0
        return remote(lambda: t_part(t_hbm, None, side, c, j), lambda: t_part(t_nb, None, side, c, j),
                      lambda: t_send.at[k, j], lambda: t_recv.at[side, j, 0], pair=lambda: z + way)

    def t_in(side, j):
        return remote(lambda: t_part(t_nb, None, side, c, j), lambda: t_part(t_nb, None, side, c, j),
                      lambda: t_send.at[side, j], lambda: t_recv.at[side, j, 0],
                      pair=lambda: z + (1 if side == 0 else -1))

    def t_across(side, j, delta, who):
        return remote(lambda: t_part(t_nb, None, side, who, j), lambda: t_part(t_nb, None, side, who, j),
                      lambda: t_fwd.at[side, j, delta], lambda: t_recv.at[side, j, delta],
                      occ=lambda: lax.rem(c + delta, n_occ))

    def t_forward(j):
        for side, (has, _) in enumerate(sides):
            arrive(t_in(side, j), has)
            for delta in range(1, n_occ):
                begin(t_across(side, j, delta, c), has)

    def t_ready(side, j, has):
        for delta in range(1, n_occ):
            arrive(t_across(side, j, delta, lax.rem(c - delta + n_occ, n_occ)), has)

    def info_hop(k):
        way = 1 if k == 0 else -1
        return remote(lambda: info, lambda: info_in.at[1 - k], lambda: info_send.at[k],
                      lambda: info_recv.at[1 - k], pair=lambda: z + way)

    def select(which, ket_at, cnt_at):
        col = lax.broadcasted_iota(jnp.int32, (width, nbas), 1) - lax.broadcasted_iota(jnp.int32, (width, nbas), 0)

        @pl.loop(0, shells)
        def _(b):
            for s in range(slots):
                at = pl.multiple_of(b * span + s * width, width)
                hit = jnp.logical_and(col == ket_at(b, s) * width, cnt_at(b) > s)
                pick[which, pl.ds(at, width), :] = jnp.where(hit, 1.0, 0.0).astype(jnp.bfloat16)

    def gather(which):
        block = 256

        @pl.loop(0, shells * span // block)
        def _(i):
            at = pl.ds(pl.multiple_of(i * block, block), block)
            weights[which, at, :] = jnp.dot(
                pick[which, at, :], coefs[...], preferred_element_type=jnp.float32).astype(jnp.bfloat16)

    def ket_rows(which, b):
        return weights[which, pl.ds(pl.multiple_of(b * span, span), span), :]

    for k, (has, way) in enumerate(sides):
        begin(hop(z, way, 0), has)
    for k, (has, way) in enumerate(sides):
        begin(info_hop(k), has)
    select(2, lambda b, s: ket[b, s], lambda b: cnt[b])
    for s in range(n_pair - 1):
        for k, (has, way) in enumerate(sides):
            owner = z - way * (s + 1)
            here = (owner >= 0) if way > 0 else (owner < n_pair)
            arrive(hop(owner, way, s), here)
            if s < n_pair - 2:
                begin(hop(owner, way, s + 1), jnp.logical_and(here, has))
            for delta in range(1, n_aux):
                begin(across(owner, k, s, delta), here)
        if s == 0:
            for j in range(chunks):
                for k, (has, way) in enumerate(sides):
                    begin(t_hop(k, j), has)
    for side, (has, way) in enumerate(sides):
        @pl.when(has)
        def _():
            info_hop(1 - side)().wait_recv()
            move = pltpu.make_async_copy(info_in.at[side], info_s.at[side], local_sem.at[1 + side])
            move.start()
            move.wait()
            select(side, lambda b, s: info_s[side, b, s], lambda b: info_s[side, b, slots])
    for s in range(n_pair - 1):
        for k, (has, way) in enumerate(sides):
            owner = z - way * (s + 1)
            here = (owner >= 0) if way > 0 else (owner < n_pair)
            for delta in range(1, n_aux):
                arrive(across_in(owner, k, s, delta), here)

    gather(2)
    local.wait()

    @pl.loop(0, shells)
    def _(b):
        w = ket_rows(2, b)

        @pl.loop(0, 2)
        def _(r):
            at = pl.multiple_of(r * half_rows, half_rows)
            half[b, pl.ds(at, half_rows), :] = jnp.dot(
                t_own[b, pl.ds(at, half_rows), :], w, preferred_element_type=jnp.float32).astype(jnp.bfloat16)

    tiles[...] = jnp.zeros_like(tiles)
    unroll = 4

    def pages(ref, at):
        return ref[:, pl.ds(pl.multiple_of(at, width), width), :].reshape(functions, orbitals)

    def own_part(lo, hi):
        def body(i, acc):
            for u in range(unroll):
                a = pages(half, (lo + i * unroll + u) * width)
                acc = acc + lax.dot_general(a, a, NT, preferred_element_type=jnp.float32)
            return acc
        zero = jnp.zeros((functions, functions), jnp.float32)
        tiles[:, functions:2 * functions] += lax.fori_loop(0, (hi - lo) // unroll, body, zero)

    n_aux_rows = rows // width
    t_forward(0)
    own_part(0, n_aux_rows // 2)
    for side, (has, way) in enumerate(sides):
        @pl.when(has)
        def _():
            gather(side)
    if chunks > 1:
        t_forward(1)
    own_part(n_aux_rows // 2, n_aux_rows)
    for j in range(chunks):
        for side, (has, way) in enumerate(sides):
            t_ready(side, j, has)

            @pl.when(has)
            def _():
                at = side * half_rows + j * step

                @pl.loop(0, shells)
                def _(b):
                    half_nb[b] = jnp.dot(t_nb[b, at:at + step, :], ket_rows(side, b),
                                         preferred_element_type=jnp.float32).astype(jnp.bfloat16)

                def body(i, acc):
                    for u in range(unroll):
                        p = i * unroll + u
                        a = pages(half, at + p * width)
                        acc = acc + lax.dot_general(a, pages(half_nb, p * width), NT,
                                                    preferred_element_type=jnp.float32)
                    return acc
                zero = jnp.zeros((functions, functions), jnp.float32)
                col = 2 * functions if side == 0 else 0
                tiles[:, col:col + functions] += lax.fori_loop(0, step // width // unroll, body, zero)
        if j + 2 < chunks:
            t_forward(j + 2)
    flips[0] = tiles[:, 2 * functions:].T
    flips[1] = tiles[:, :functions].T

    def cut(ref, r):
        return ref.at[pl.ds(pl.multiple_of(r * out_rows, out_rows), out_rows), :]

    def same(delta):
        other = lax.rem(mine + delta, n_red)
        return remote(lambda: cut(tiles, other), lambda: red_same.at[delta], lambda: same_send.at[delta],
                      lambda: same_recv.at[delta], aux=lambda: other // n_occ, occ=lambda: lax.rem(other, n_occ))

    def cross(side, delta):
        other = lax.rem(mine + delta, n_red)
        way = 1 if side == 0 else -1
        return remote(lambda: cut(flips.at[side], other), lambda: red_cross.at[side, delta],
                      lambda: cross_send.at[side, delta], lambda: cross_recv.at[side, delta],
                      pair=lambda: z + way, aux=lambda: other // n_occ, occ=lambda: lax.rem(other, n_occ))

    for delta in range(n_red):
        for side, (has, way) in enumerate(sides):
            begin(cross(side, delta), has)
    for delta in range(1, n_red):
        begin(same(delta))

    total = tiles[pl.ds(pl.multiple_of(mine * out_rows, out_rows), out_rows), :]
    for delta in range(1, n_red):
        arrive(same(delta))
        total = total + red_same[delta]
    tiles_out = [total[:, i * functions:(i + 1) * functions] for i in range(3)]
    for side, (has, way) in enumerate(sides):
        comes = has_down if side == 0 else has_up
        for delta in range(n_red):
            arrive(cross(side, delta), comes)
        col = 0 if side == 0 else 2
        more = red_cross[side, 0]
        for delta in range(1, n_red):
            more = more + red_cross[side, delta]
        tiles_out[col] = jnp.where(comes, tiles_out[col] + more, 0.0)

    scale = 1.0 / math.sqrt(n_aux_rows * n_aux * orbitals * n_occ)
    r_id = lax.broadcasted_iota(jnp.int32, (out_rows, functions), 0) + mine * out_rows
    c_id = lax.broadcasted_iota(jnp.int32, (out_rows, functions), 1)
    r_size = jnp.zeros_like(r_id)
    for b in range(shells):
        r_size = jnp.where(r_id // width == b, size[b], r_size)
    r_live = lax.rem(r_id, width) < r_size
    for i in range(3):
        c_size = jnp.zeros_like(c_id)
        for b in range(shells):
            there = size[b] if i == 1 else info_s[1 if i == 0 else 0, b, slots + 1]
            c_size = jnp.where(c_id // width == b, there, c_size)
        live = jnp.logical_and(r_live, lax.rem(c_id, width) < c_size)
        out[:, i * functions:(i + 1) * functions] = jnp.where(live, tiles_out[i] * scale, 0.0)

    for cond, make in pending:
        when(cond, make, lambda d: d.wait_send())


def shards(chunks, three_index, coefficients, shell_size, ket_shell, ket_count):
    shells, aux_rows, width, span = three_index.shape
    slots = span // width
    n_pair, n_aux, n_occ = (lax.axis_size(a) for a in ("pair", "aux", "occ"))
    n_red = n_aux * n_occ
    orbitals = coefficients.shape[1]
    functions = shells * width
    rows = aux_rows * width
    out_rows = functions // n_red
    step = rows // 2 // chunks
    bf16, f32 = jnp.bfloat16, jnp.float32
    dma = pltpu.SemaphoreType.DMA
    smem = pl.BlockSpec(memory_space=pltpu.SMEM)
    vmem = pl.BlockSpec(memory_space=pltpu.VMEM)
    return pl.pallas_call(
        functools.partial(kernel, (n_pair, n_aux, n_occ, width, slots, chunks)),
        out_shape=jax.ShapeDtypeStruct((out_rows, 3 * functions), f32),
        in_specs=[pl.BlockSpec(memory_space=pl.ANY), vmem, smem, smem, smem],
        out_specs=vmem,
        scratch_shapes=[
            pltpu.VMEM((shells, rows, span), bf16),
            pltpu.VMEM((shells, rows, span), bf16),
            pltpu.VMEM((n_pair * functions, orbitals), bf16),
            pltpu.VMEM((3, shells * span, n_pair * functions), bf16),
            pltpu.VMEM((3, shells * span, orbitals), bf16),
            pltpu.VMEM((shells, rows, orbitals), bf16),
            pltpu.VMEM((shells, step, orbitals), bf16),
            pltpu.VMEM((shells, 128), jnp.int32),
            pltpu.VMEM((2, shells, 128), jnp.int32),
            pltpu.SMEM((2, shells, 128), jnp.int32),
            pltpu.VMEM((functions, 3 * functions), f32),
            pltpu.VMEM((2, functions, functions), f32),
            pltpu.VMEM((n_red, out_rows, 3 * functions), f32),
            pltpu.VMEM((2, n_red, out_rows, functions), f32),
            dma((3,)),
            dma((2, n_pair)),
            dma((2, n_pair, n_aux)),
            dma((2, n_pair, n_aux)),
            dma((2,)),
            dma((2,)),
            dma((2, chunks)),
            dma((2, chunks, n_occ)),
            dma((2, chunks, n_occ)),
            dma((n_red,)),
            dma((n_red,)),
            dma((2, n_red)),
            dma((2, n_red)),
        ],
        compiler_params=pltpu.CompilerParams(
            collective_id=0, has_side_effects=True, vmem_limit_bytes=48 * 1024 * 1024),
    )(three_index.reshape(shells, rows, span), coefficients, shell_size, ket_shell, ket_count)


def solution(mesh):
    return jax.shard_map(
        functools.partial(shards, 4),
        mesh=mesh,
        in_specs=(
            P(("parts", "pair"), "aux", None, None),
            P(("parts", "pair"), "occ"),
            P(("parts", "pair")),
            P(("parts", "pair"), None),
            P(("parts", "pair")),
        ),
        out_specs=P(("parts", "pair", "aux", "occ"), None),
        check_vma=False,
    )
```

time: 313 us -> 57.7 us (0.18)
  waiting for transfers between devices: 201 us -> 0 us
  Pallas kernels: 0 us -> 52.4 us
  matrix products: 44.6 us -> 0 us
  blocking collectives: 17.4 us -> 0 us
  local copies, waits for them, and re-layouts: 19.3 us -> 5.11 us
  between operations: 13.5 us -> 0.01 us
  other arithmetic: 13.1 us -> 0 us
    ppermute x2 -> x0, waiting for transfers between devices: 182 us -> none  [passed_along(): return lax.ppermute(x, axis, pairs)]
    pallas_call x0 -> x1, Pallas kernels: none -> 52.4 us  [shards(): pl.pallas_call(functools.partial(kernel, (n_pair, n_aux, n_occ, width, sl...]
    dot_general x10 -> x0, matrix products: 44.6 us -> none  [the longest x8 19.5 us: one_shell(): jnp.dot(block.reshape(aux_rows * width, span), rows, preferred_element_ty...]
    reduce_scatter x1 -> x0, waiting for transfers between devices: 19.3 us -> none  [shards(): lax.psum_scatter(tiles, ('aux', 'occ'), scatter_dimension=0, tiled=True)]
    all_gather x1 -> x0, blocking collectives: 17.4 us -> none  [shards(): whole = lax.all_gather(coef_masked, 'pair', axis=0, tiled=True)]
    dynamic_slice x8 -> x0, local copies, waits for them, and re-layouts: 9.68 us -> none  [shards(): half = lax.map(one_shell, (ket_shell, ket_count, three_index, shell_mask))]
    gather x8 -> x0, local copies, waits for them, and re-layouts: 6.8 us -> none  [one_shell(): rows = whole[index]]
    mul x8 -> x0, other arithmetic: 5.54 us -> none  [one_shell(): index = (kets[:, None] * width + lanes[None, :]).reshape(slots * width)]
  transfers between devices with their start and end apart: 3 -> 0, of which waited for: 2 -> 0; matrix products, arithmetic and copies ran while one was open for 4% -> 0% of each run, Pallas kernels for 0% -> 0%
where the time goes in v1:
time: 57.7 us; the launch traced here: 57.5 us
  Pallas kernels  52.4 us (91%)
  local copies, waits for them, and re-layouts  5.11 us (9%)
    pallas_call x1, Pallas kernels, shards(): pl.pallas_call(functools.partial(kernel, (n_pair, n_aux, n_occ, width, sl...  52.4 us
    unnamed x11, local copies, waits for them, and re-layouts  5.11 us

profile of v1, /device:TPU:0, one launch (start us, length us, event | category | flops | bytes accessed | tf_op | source)
XLA Modules:
  0.0 57.5 jit_solution(17418290829014276585)
XLA Ops:
  0.0 0.0 copy-start
  0.0 1.6 %copy-done = bf16[8,64,16,128]{3,2,1,0:T(8,128)(2,1)S(1)} copy-done((bf16[8,64,16,128]{3,2,1,0:T(8,128)(2,1)S(1)}, bf16[8,64,16,128]{3,2,1,0:T(8,128)(2,1)}, u32[]{:S(2)}) %copy-start) | copy-done | bytes 2097176
  1.6 0.0 copy-start.1
  1.6 0.9 %copy-done.1 = bf16[128,512]{1,0:T(8,128)(2,1)S(1)} copy-done((bf16[128,512]{1,0:T(8,128)(2,1)S(1)}, bf16[128,512]{1,0:T(8,128)(2,1)}, u32[]{:S(2)}) %copy-start.1) | copy-done | bytes 131096
  2.5 0.0 copy-start.2
  2.5 0.7 %copy-done.2 = s32[8,8]{1,0:T(8,128)S(1)} copy-done((s32[8,8]{1,0:T(8,128)S(1)}, s32[8,8]{1,0:T(8,128)}, u32[]{:S(2)}) %copy-start.2) | copy-done | bytes 280
  3.2 0.0 copy-start.3
  3.2 0.7 %copy-done.3 = s32[8]{0:T(128)S(1)} copy-done((s32[8]{0:T(128)S(1)}, s32[8]{0:T(128)}, u32[]{:S(2)}) %copy-start.3) | copy-done | bytes 56
  3.8 0.0 copy-start.4
  3.8 0.7 %copy-done.4 = s32[8]{0:T(128)S(1)} copy-done((s32[8]{0:T(128)S(1)}, s32[8]{0:T(128)}, u32[]{:S(2)}) %copy-start.4) | copy-done | bytes 56
  4.5 52.4 %shard_map.55 = f32[32,384]{1,0:T(8,128)S(1)} custom-call(bf16[8,1024,128]{2,1,0:T(8,128)(2,1)S(1)} %bitcast.1, bf16[128,512]{1,0:T(8,128)(2,1)S(1)} %copy-done.1, s32[8]{0:T(128)S(1)} %copy-done.3, s32[8,8]{1,0:T(8,128)S(1)} %copy-done.2, s32[8]{0:T(128)S(1)} %copy-done.4), custom_call_target="tpu_custom_call" | custom-call | tf_op jit(solution)/shard_map/pallas_call | solution.py:336
  56.9 0.6 %copy.7 = f32[32,384]{1,0:T(8,128)} copy(f32[32,384]{1,0:T(8,128)S(1)} %shard_map.55) | data formatting | bytes 98304
Async XLA Ops:
  0.0 1.6 %copy-start = (bf16[8,64,16,128]{3,2,1,0:T(8,128)(2,1)S(1)}, bf16[8,64,16,128]{3,2,1,0:T(8,128)(2,1)}, u32[]{:S(2)}) copy-start(bf16[8,64,16,128]{3,2,1,0:T(8,128)(2,1)} %param.5) | copy-start | bytes 6291460
  1.6 0.9 %copy-start.1 = (bf16[128,512]{1,0:T(8,128)(2,1)S(1)}, bf16[128,512]{1,0:T(8,128)(2,1)}, u32[]{:S(2)}) copy-start(bf16[128,512]{1,0:T(8,128)(2,1)} %coef.1) | copy-start | bytes 393220
  2.5 0.7 %copy-start.2 = (s32[8,8]{1,0:T(8,128)S(1)}, s32[8,8]{1,0:T(8,128)}, u32[]{:S(2)}) copy-start(s32[8,8]{1,0:T(8,128)} %ket.1) | copy-start | bytes 772
  3.2 0.7 %copy-start.3 = (s32[8]{0:T(128)S(1)}, s32[8]{0:T(128)}, u32[]{:S(2)}) copy-start(s32[8]{0:T(128)} %size.1) | copy-start | bytes 100
  3.8 0.7 %copy-start.4 = (s32[8]{0:T(128)S(1)}, s32[8]{0:T(128)}, u32[]{:S(2)}) copy-start(s32[8]{0:T(128)} %cnt.1) | copy-start | bytes 100

commit v2 on v1

v2 whole, which is shorter than its diff:
```python
import functools
import math

import jax
import jax.numpy as jnp
from jax import lax
from jax.experimental import pallas as pl
from jax.experimental.pallas import tpu as pltpu
from jax.sharding import PartitionSpec as P

MESH = pl.DeviceIdType.MESH
NT = (((1,), (1,)), ((), ()))


def kernel(sizes, t_hbm, coef_hbm, size_hbm, ket_hbm, cnt_hbm, out, coef, size, ket, cnt, t_own, t_nb, coefs, pick, density, weights, left, spread, spread_nb, info,
           info_in, info_s, tiles, flips, red_same, red_cross, local_sem, coef_send, coef_recv, coef_fwd, coef_cross,
           info_send, info_recv, t_send, t_recv, same_send, same_recv, cross_send, cross_recv):
    n_pair, n_aux, n_occ, width, slots, chunks = sizes
    shells, rows, span = t_own.shape
    orbitals = coef.shape[1]
    functions = shells * width
    n_red = n_aux * n_occ
    half_rows = rows // 2
    step = half_rows // chunks
    out_rows = functions // n_red
    top = width * 5 // 8
    kept = shells * top
    nbas = coefs.shape[0]
    z = lax.axis_index("pair")
    x = lax.axis_index("aux")
    c = lax.axis_index("occ")
    mine = x * n_occ + c
    base = pl.multiple_of(c * rows, rows)
    has_up = z + 1 < n_pair
    has_down = z > 0
    sides = ((has_up, 1), (has_down, -1))
    pending = []

    def when(cond, make, act):
        if cond is None:
            act(make())
        else:
            @pl.when(cond)
            def _():
                act(make())

    def begin(make, cond=None):
        when(cond, make, lambda d: d.start())
        pending.append((cond, make))

    def arrive(make, cond=None):
        when(cond, make, lambda d: d.wait_recv())

    def remote(src, dst, s_sem, r_sem, **where):
        return lambda: pltpu.make_async_remote_copy(
            src_ref=src(), dst_ref=dst(), send_sem=s_sem(), recv_sem=r_sem(),
            device_id={k: v() for k, v in where.items()}, device_id_type=MESH)

    local = pltpu.make_async_copy(t_hbm.at[:, pl.ds(base, rows), :], t_own, local_sem.at[0])
    small = [pltpu.make_async_copy(src, dst, local_sem.at[3 + i]) for i, (src, dst) in enumerate(
        ((size_hbm, size), (coef_hbm, coef), (ket_hbm, ket), (cnt_hbm, cnt)))]
    for move in small:
        move.start()
    local.start()

    barrier = pltpu.get_barrier_semaphore()
    for delta in range(n_red):
        other = lax.rem(mine + delta, n_red)
        ox, oc = other // n_occ, lax.rem(other, n_occ)
        if delta > 0:
            pl.semaphore_signal(barrier, inc=1, device_id={"aux": ox, "occ": oc}, device_id_type=MESH)
        for has, way in sides:
            @pl.when(has)
            def _():
                pl.semaphore_signal(
                    barrier, inc=1, device_id={"pair": z + way, "aux": ox, "occ": oc}, device_id_type=MESH)

    for move in small:
        move.wait()
    fun = lax.broadcasted_iota(jnp.int32, (width, orbitals), 0)
    masked = jnp.concatenate([
        jnp.where(fun < size[b], coef[b * width:(b + 1) * width, :].astype(jnp.float32), 0.0)
        for b in range(shells)], axis=0).astype(jnp.bfloat16)
    to = lax.broadcasted_iota(jnp.int32, (kept, functions), 0)
    frm = lax.broadcasted_iota(jnp.int32, (kept, functions), 1)
    g = lax.rem(frm, width)
    packing = jnp.logical_and(to == (frm // width) * top + g, g < top)
    packing = jnp.where(packing, 1.0, 0.0).astype(jnp.bfloat16)
    mine_cols = pl.ds(pl.multiple_of(c * orbitals, orbitals), orbitals)
    coefs[pl.ds(pl.multiple_of(z * kept, kept), kept), mine_cols] = jnp.dot(
        packing, masked, preferred_element_type=jnp.float32).astype(jnp.bfloat16)
    if nbas > n_pair * kept:
        coefs[n_pair * kept:, :] = jnp.zeros((nbas - n_pair * kept, n_occ * orbitals), jnp.bfloat16)

    row = lax.broadcasted_iota(jnp.int32, info.shape, 0)
    lane = lax.broadcasted_iota(jnp.int32, info.shape, 1)
    packed = jnp.zeros(info.shape, jnp.int32)
    for b in range(shells):
        line = jnp.where(lane == slots, cnt[b], jnp.where(lane == slots + 1, size[b], 0))
        for s in range(slots):
            line = jnp.where(lane == s, ket[b, s], line)
        packed = jnp.where(row == b, line, packed)
    info[...] = packed

    ups, downs = has_up.astype(jnp.int32), has_down.astype(jnp.int32)
    pl.semaphore_wait(barrier, n_red - 1 + n_red * (ups + downs))

    def part(owner, who):
        return coefs.at[pl.ds(pl.multiple_of(owner * kept, kept), kept),
                        pl.ds(pl.multiple_of(who * orbitals, orbitals), orbitals)]

    def hop(owner, way, s):
        k = 0 if way > 0 else 1
        return remote(lambda: part(owner, c), lambda: part(owner, c), lambda: coef_send.at[k, s],
                      lambda: coef_recv.at[k, s], pair=lambda: z + way)

    def across(owner, k, s, delta, who):
        return remote(lambda: part(owner, who), lambda: part(owner, who), lambda: coef_fwd.at[k, s, delta],
                      lambda: coef_cross.at[k, s, delta], occ=lambda: lax.rem(c + delta, n_occ))

    def across_in(owner, k, s, delta):
        return across(owner, k, s, delta, lax.rem(c - delta + n_occ, n_occ))

    def t_hop(k, j):
        way, side = (1, 1) if k == 0 else (-1, 0)
        at = side * half_rows + j * step
        return remote(lambda: t_hbm.at[:, pl.ds(base + at, step), :], lambda: t_nb.at[:, pl.ds(at, step), :],
                      lambda: t_send.at[k, j], lambda: t_recv.at[side, j], pair=lambda: z + way)

    def info_hop(k):
        way = 1 if k == 0 else -1
        return remote(lambda: info, lambda: info_in.at[1 - k], lambda: info_send.at[k],
                      lambda: info_recv.at[1 - k], pair=lambda: z + way)

    def select(which, ket_at, cnt_at):
        col = lax.broadcasted_iota(jnp.int32, (width, nbas), 1) - lax.broadcasted_iota(jnp.int32, (width, nbas), 0)
        live = lax.broadcasted_iota(jnp.int32, (width, nbas), 0) < top

        @pl.loop(0, shells)
        def _(b):
            for s in range(slots):
                at = pl.multiple_of(b * span + s * width, width)
                hit = jnp.logical_and(jnp.logical_and(col == ket_at(b, s) * top, live), cnt_at(b) > s)
                pick[which, pl.ds(at, width), :] = jnp.where(hit, 1.0, 0.0).astype(jnp.bfloat16)

    def picked(which, b):
        return pick[which, pl.ds(pl.multiple_of(b * span, span), span), :]

    def scatter(which, lo, hi):
        @pl.loop(lo, hi)
        def _(b):
            spread[b] = jnp.dot(t_own[b], picked(which, b), preferred_element_type=jnp.float32).astype(jnp.bfloat16)

    for k, (has, way) in enumerate(sides):
        begin(hop(z, way, 0), has)
    for delta in range(1, n_occ):
        begin(across(z, 0, n_pair - 1, delta, c))
    for k, (has, way) in enumerate(sides):
        begin(info_hop(k), has)
    select(2, lambda b, s: ket[b, s], lambda b: cnt[b])
    local.wait()
    for s in range(n_pair - 1):
        for k, (has, way) in enumerate(sides):
            owner = z - way * (s + 1)
            here = (owner >= 0) if way > 0 else (owner < n_pair)
            arrive(hop(owner, way, s), here)
            if s < n_pair - 2:
                begin(hop(owner, way, s + 1), jnp.logical_and(here, has))
            for delta in range(1, n_occ):
                begin(across(owner, k, s, delta, c), here)
        if s == 0:
            for j in range(chunks):
                for k, (has, way) in enumerate(sides):
                    begin(t_hop(k, j), has)
            scatter(2, 0, shells // 2)
        if s == 1 or n_pair == 2:
            scatter(2, shells // 2, shells)
    for delta in range(1, n_occ):
        arrive(across_in(z, 0, n_pair - 1, delta))
    for s in range(n_pair - 1):
        for k, (has, way) in enumerate(sides):
            owner = z - way * (s + 1)
            here = (owner >= 0) if way > 0 else (owner < n_pair)
            for delta in range(1, n_occ):
                arrive(across_in(owner, k, s, delta), here)

    lines = 128

    @pl.loop(0, nbas // lines)
    def _(i):
        at = pl.ds(pl.multiple_of(i * lines, lines), lines)
        d = lax.dot_general(coefs[at, :], coefs[...], NT, preferred_element_type=jnp.float32)
        high = d.astype(jnp.bfloat16)
        density[0, at, :] = high
        density[1, at, :] = (d - high.astype(jnp.float32)).astype(jnp.bfloat16)

    for part_id in range(2):
        @pl.loop(0, shells)
        def _(b):
            weights[b, part_id * span:(part_id + 1) * span, :] = jnp.dot(
                picked(2, b), density[part_id], preferred_element_type=jnp.float32).astype(jnp.bfloat16)

    @pl.loop(0, shells)
    def _(b):
        t = t_own[b]
        left[b] = jnp.dot(jnp.concatenate([t, t], axis=1), weights[b],
                          preferred_element_type=jnp.float32).astype(jnp.bfloat16)

    tiles[...] = jnp.zeros_like(tiles)
    unroll = 4

    def pages(ref, at):
        return ref[:, pl.ds(pl.multiple_of(at, width), width), :].reshape(functions, nbas)

    def contract(other, at, count, off, col):
        def body(i, acc):
            for u in range(unroll):
                p = (i * unroll + u) * width
                acc = acc + lax.dot_general(pages(left, at + p), pages(other, p + off), NT,
                                            preferred_element_type=jnp.float32)
            return acc
        zero = jnp.zeros((functions, functions), jnp.float32)
        tiles[:, col:col + functions] += lax.fori_loop(0, count // width // unroll, body, zero)

    contract(spread, 0, rows, 0, functions)
    for side, (has, way) in enumerate(sides):
        @pl.when(has)
        def _():
            info_hop(1 - side)().wait_recv()
            move = pltpu.make_async_copy(info_in.at[side], info_s.at[side], local_sem.at[1 + side])
            move.start()
            move.wait()
            select(side, lambda b, s: info_s[side, b, s], lambda b: info_s[side, b, slots])
    for j in range(chunks):
        for side, (has, way) in enumerate(sides):
            @pl.when(has)
            def _():
                t_hop(1 - side, j)().wait_recv()
                at = side * half_rows + j * step

                @pl.loop(0, shells)
                def _(b):
                    spread_nb[b] = jnp.dot(t_nb[b, at:at + step, :], picked(side, b),
                                           preferred_element_type=jnp.float32).astype(jnp.bfloat16)
                contract(spread_nb, at, step, 0, 2 * functions if side == 0 else 0)
    flips[0] = tiles[:, 2 * functions:].T
    flips[1] = tiles[:, :functions].T

    def cut(ref, r):
        return ref.at[pl.ds(pl.multiple_of(r * out_rows, out_rows), out_rows), :]

    def same(delta):
        other = lax.rem(mine + delta, n_red)
        return remote(lambda: cut(tiles, other), lambda: red_same.at[delta], lambda: same_send.at[delta],
                      lambda: same_recv.at[delta], aux=lambda: other // n_occ, occ=lambda: lax.rem(other, n_occ))

    def cross(side, delta):
        other = lax.rem(mine + delta, n_red)
        way = 1 if side == 0 else -1
        return remote(lambda: cut(flips.at[side], other), lambda: red_cross.at[side, delta],
                      lambda: cross_send.at[side, delta], lambda: cross_recv.at[side, delta],
                      pair=lambda: z + way, aux=lambda: other // n_occ, occ=lambda: lax.rem(other, n_occ))

    for delta in range(n_red):
        for side, (has, way) in enumerate(sides):
            begin(cross(side, delta), has)
    for delta in range(1, n_red):
        begin(same(delta))

    total = tiles[pl.ds(pl.multiple_of(mine * out_rows, out_rows), out_rows), :]
    for delta in range(1, n_red):
        arrive(same(delta))
        total = total + red_same[delta]
    tiles_out = [total[:, i * functions:(i + 1) * functions] for i in range(3)]
    for side, (has, way) in enumerate(sides):
        comes = has_down if side == 0 else has_up
        for delta in range(n_red):
            arrive(cross(side, delta), comes)
        col = 0 if side == 0 else 2
        more = red_cross[side, 0]
        for delta in range(1, n_red):
            more = more + red_cross[side, delta]
        tiles_out[col] = jnp.where(comes, tiles_out[col] + more, 0.0)

    scale = 1.0 / math.sqrt(rows // width * n_red * orbitals * n_occ)
    r_id = lax.broadcasted_iota(jnp.int32, (out_rows, functions), 0) + mine * out_rows
    c_id = lax.broadcasted_iota(jnp.int32, (out_rows, functions), 1)
    r_size = jnp.zeros_like(r_id)
    for b in range(shells):
        r_size = jnp.where(r_id // width == b, size[b], r_size)
    r_live = lax.rem(r_id, width) < r_size
    for i in range(3):
        c_size = jnp.zeros_like(c_id)
        for b in range(shells):
            there = size[b] if i == 1 else info_s[1 if i == 0 else 0, b, slots + 1]
            c_size = jnp.where(c_id // width == b, there, c_size)
        live = jnp.logical_and(r_live, lax.rem(c_id, width) < c_size)
        out[:, i * functions:(i + 1) * functions] = jnp.where(live, tiles_out[i] * scale, 0.0)

    for cond, make in pending:
        when(cond, make, lambda d: d.wait_send())


def shards(chunks, three_index, coefficients, shell_size, ket_shell, ket_count):
    shells, aux_rows, width, span = three_index.shape
    slots = span // width
    n_pair, n_aux, n_occ = (lax.axis_size(a) for a in ("pair", "aux", "occ"))
    n_red = n_aux * n_occ
    orbitals = coefficients.shape[1]
    functions = shells * width
    rows = aux_rows * width // n_occ
    kept = n_pair * shells * (width * 5 // 8)
    nbas = -(-kept // 128) * 128
    out_rows = functions // n_red
    step = rows // 2 // chunks
    bf16, f32 = jnp.bfloat16, jnp.float32
    dma = pltpu.SemaphoreType.DMA
    vmem = pl.BlockSpec(memory_space=pltpu.VMEM)
    return pl.pallas_call(
        functools.partial(kernel, (n_pair, n_aux, n_occ, width, slots, chunks)),
        out_shape=jax.ShapeDtypeStruct((out_rows, 3 * functions), f32),
        in_specs=[pl.BlockSpec(memory_space=pl.ANY)] * 5,
        out_specs=vmem,
        scratch_shapes=[
            pltpu.VMEM((functions, orbitals), bf16),
            pltpu.SMEM((shells,), jnp.int32),
            pltpu.SMEM((shells, slots), jnp.int32),
            pltpu.SMEM((shells,), jnp.int32),
            pltpu.VMEM((shells, rows, span), bf16),
            pltpu.VMEM((shells, rows, span), bf16),
            pltpu.VMEM((nbas, n_occ * orbitals), bf16),
            pltpu.VMEM((3, shells * span, nbas), bf16),
            pltpu.VMEM((2, nbas, nbas), bf16),
            pltpu.VMEM((shells, 2 * span, nbas), bf16),
            pltpu.VMEM((shells, rows, nbas), bf16),
            pltpu.VMEM((shells, rows, nbas), bf16),
            pltpu.VMEM((shells, step, nbas), bf16),
            pltpu.VMEM((shells, 128), jnp.int32),
            pltpu.VMEM((2, shells, 128), jnp.int32),
            pltpu.SMEM((2, shells, 128), jnp.int32),
            pltpu.VMEM((functions, 3 * functions), f32),
            pltpu.VMEM((2, functions, functions), f32),
            pltpu.VMEM((n_red, out_rows, 3 * functions), f32),
            pltpu.VMEM((2, n_red, out_rows, functions), f32),
            dma((7,)),
            dma((2, n_pair)),
            dma((2, n_pair)),
            dma((2, n_pair, n_occ)),
            dma((2, n_pair, n_occ)),
            dma((2,)),
            dma((2,)),
            dma((2, chunks)),
            dma((2, chunks)),
            dma((n_red,)),
            dma((n_red,)),
            dma((2, n_red)),
            dma((2, n_red)),
        ],
        compiler_params=pltpu.CompilerParams(
            collective_id=0, has_side_effects=True, vmem_limit_bytes=64 * 1024 * 1024),
    )(three_index.reshape(shells, aux_rows * width, span), coefficients, shell_size, ket_shell, ket_count)


def solution(mesh):
    return jax.shard_map(
        functools.partial(shards, 2),
        mesh=mesh,
        in_specs=(
            P(("parts", "pair"), "aux", None, None),
            P(("parts", "pair"), "occ"),
            P(("parts", "pair")),
            P(("parts", "pair"), None),
            P(("parts", "pair")),
        ),
        out_specs=P(("parts", "pair", "aux", "occ"), None),
        check_vma=False,
    )
```

time: 57.7 us -> 46.4 us (0.80)
  Pallas kernels: 52.4 us -> 44.8 us
  local copies, waits for them, and re-layouts: 5.11 us -> 1.42 us
    pallas_call x1, Pallas kernels: 52.4 us -> 44.8 us  [shards(): pl.pallas_call(functools.partial(kernel, (n_pair, n_aux, n_occ, width, sl...]
    unnamed x11 -> x1, local copies, waits for them, and re-layouts: 5.11 us -> 1.42 us
where the time goes in v2:
time: 46.4 us; the launch traced here: 46.2 us
  Pallas kernels  44.8 us (97%)
  local copies, waits for them, and re-layouts  1.42 us (3%)
    pallas_call x1, Pallas kernels, shards(): pl.pallas_call(functools.partial(kernel, (n_pair, n_aux, n_occ, width, sl...  44.8 us
    unnamed x1, local copies, waits for them, and re-layouts  1.42 us

profile of v2, /device:TPU:0, one launch (start us, length us, event | category | flops | bytes accessed | tf_op | source)
XLA Modules:
  0.0 46.2 jit_solution(8106635772440433733)
XLA Ops:
  0.0 44.8 %shard_map.55 = f32[32,384]{1,0:T(8,128)} custom-call(bf16[8,1024,128]{2,1,0:T(8,128)(2,1)} %bitcast.1, bf16[128,512]{1,0:T(8,128)(2,1)} %coef_hbm.1, s32[8]{0:T(128)} %size_hbm.1, s32[8,8]{1,0:T(8,128)} %ket_hbm.1, s32[8]{0:T(128)} %cnt_hbm.1), custom_call_target="tpu_custom_call" | custom-call | tf_op jit(solution)/shard_map/pallas_call | solution.py:319
  44.8 1.4 %copy.7 = f32[32,384]{1,0:T(8,128)} copy(f32[32,384]{1,0:T(8,128)} %shard_map.55) | data formatting | bytes 98304

commit v3 on v2

--- a/solution.py
+++ b/solution.py
@@ -12,7 +12,7 @@
 NT = (((1,), (1,)), ((), ()))
 
 
-def kernel(sizes, t_hbm, coef_hbm, size_hbm, ket_hbm, cnt_hbm, out, coef, size, ket, cnt, t_own, t_nb, coefs, pick, density, weights, left, spread, spread_nb, info,
+def kernel(sizes, t_hbm, coef_hbm, size_hbm, ket_hbm, cnt_hbm, out, coef, size, ket, cnt, t_own, t_nb, coefs, pick, narrow, widen, t_pack, density, weights, left, spread, spread_nb, info,
            info_in, info_s, tiles, flips, red_same, red_cross, local_sem, coef_send, coef_recv, coef_fwd, coef_cross,
            info_send, info_recv, t_send, t_recv, same_send, same_recv, cross_send, cross_recv):
     n_pair, n_aux, n_occ, width, slots, chunks = sizes
@@ -85,10 +85,15 @@
     frm = lax.broadcasted_iota(jnp.int32, (kept, functions), 1)
     g = lax.rem(frm, width)
     packing = jnp.logical_and(to == (frm // width) * top + g, g < top)
-    packing = jnp.where(packing, 1.0, 0.0).astype(jnp.bfloat16)
+    narrow[...] = jnp.where(packing, 1.0, 0.0).astype(jnp.bfloat16)
     mine_cols = pl.ds(pl.multiple_of(c * orbitals, orbitals), orbitals)
     coefs[pl.ds(pl.multiple_of(z * kept, kept), kept), mine_cols] = jnp.dot(
-        packing, masked, preferred_element_type=jnp.float32).astype(jnp.bfloat16)
+        narrow[...], masked, preferred_element_type=jnp.float32).astype(jnp.bfloat16)
+    to = lax.broadcasted_iota(jnp.int32, (functions, kept), 1)
+    frm = lax.broadcasted_iota(jnp.int32, (functions, kept), 0)
+    g = lax.rem(frm, width)
+    packing = jnp.logical_and(to == (frm // width) * top + g, g < top)
+    widen[...] = jnp.where(packing, 1.0, 0.0).astype(jnp.bfloat16)
     if nbas > n_pair * kept:
         coefs[n_pair * kept:, :] = jnp.zeros((nbas - n_pair * kept, n_occ * orbitals), jnp.bfloat16)
 
@@ -123,8 +128,7 @@
 
     def t_hop(k, j):
         way, side = (1, 1) if k == 0 else (-1, 0)
-        at = side * half_rows + j * step
-        return remote(lambda: t_hbm.at[:, pl.ds(base + at, step), :], lambda: t_nb.at[:, pl.ds(at, step), :],
+        return remote(lambda: t_pack.at[side, j], lambda: t_nb.at[side, j],
                       lambda: t_send.at[k, j], lambda: t_recv.at[side, j], pair=lambda: z + way)
 
     def info_hop(k):
@@ -159,6 +163,15 @@
         begin(info_hop(k), has)
     select(2, lambda b, s: ket[b, s], lambda b: cnt[b])
     local.wait()
+
+    for side in range(2):
+        for j in range(chunks):
+            at = side * half_rows + j * step
+            packed = jnp.dot(narrow[...], jnp.concatenate([t_own[b, at:at + step, :] for b in range(shells)], axis=1),
+                             preferred_element_type=jnp.float32).astype(jnp.bfloat16)
+            for b in range(shells):
+                t_pack[side, j, b] = packed[:, b * span:(b + 1) * span]
+
     for s in range(n_pair - 1):
         for k, (has, way) in enumerate(sides):
             owner = z - way * (s + 1)
@@ -168,10 +181,11 @@
                 begin(hop(owner, way, s + 1), jnp.logical_and(here, has))
             for delta in range(1, n_occ):
                 begin(across(owner, k, s, delta, c), here)
-        if s == 0:
+        if s == max(n_pair - 3, 0):
             for j in range(chunks):
                 for k, (has, way) in enumerate(sides):
                     begin(t_hop(k, j), has)
+        if s == 0:
             scatter(2, 0, shells // 2)
         if s == 1 or n_pair == 2:
             scatter(2, shells // 2, shells)
@@ -184,41 +198,46 @@
             for delta in range(1, n_occ):
                 arrive(across_in(owner, k, s, delta), here)
 
-    lines = 128
+    lines = 384 if nbas % 384 == 0 else 128
 
     @pl.loop(0, nbas // lines)
     def _(i):
         at = pl.ds(pl.multiple_of(i * lines, lines), lines)
         d = lax.dot_general(coefs[at, :], coefs[...], NT, preferred_element_type=jnp.float32)
         high = d.astype(jnp.bfloat16)
-        density[0, at, :] = high
-        density[1, at, :] = (d - high.astype(jnp.float32)).astype(jnp.bfloat16)
-
-    for part_id in range(2):
-        @pl.loop(0, shells)
-        def _(b):
-            weights[b, part_id * span:(part_id + 1) * span, :] = jnp.dot(
-                picked(2, b), density[part_id], preferred_element_type=jnp.float32).astype(jnp.bfloat16)
-
-    @pl.loop(0, shells)
+        density[at, :nbas] = high
+        density[at, nbas:] = (d - high.astype(jnp.float32)).astype(jnp.bfloat16)
+
+    together = 4
+
+    @pl.loop(0, shells // together)
+    def _(i):
+        at = pl.multiple_of(i * together * span, together * span)
+        w = jnp.dot(pick[2, pl.ds(at, together * span), :], density[...],
+                    preferred_element_type=jnp.float32).astype(jnp.bfloat16)
+        w = w.reshape(together, span, 2 * nbas)
+        weights[pl.ds(i * together, together), :span, :] = w[:, :, :nbas]
+        weights[pl.ds(i * together, together), span:, :] = w[:, :, nbas:]
+
+    @pl.loop(0, shells, unroll=2)
     def _(b):
         t = t_own[b]
         left[b] = jnp.dot(jnp.concatenate([t, t], axis=1), weights[b],
                           preferred_element_type=jnp.float32).astype(jnp.bfloat16)
 
     tiles[...] = jnp.zeros_like(tiles)
-    unroll = 4
+    unroll = 8
 
     def pages(ref, at):
-        return ref[:, pl.ds(pl.multiple_of(at, width), width), :].reshape(functions, nbas)
+        return jnp.concatenate([
+            ref[:, pl.ds(pl.multiple_of(at + u * width, width), width), :].reshape(functions, nbas)
+            for u in range(unroll)], axis=1)
 
     def contract(other, at, count, off, col):
         def body(i, acc):
-            for u in range(unroll):
-                p = (i * unroll + u) * width
-                acc = acc + lax.dot_general(pages(left, at + p), pages(other, p + off), NT,
-                                            preferred_element_type=jnp.float32)
-            return acc
+            p = i * unroll * width
+            return acc + lax.dot_general(pages(left, at + p), pages(other, p + off), NT,
+                                         preferred_element_type=jnp.float32)
         zero = jnp.zeros((functions, functions), jnp.float32)
         tiles[:, col:col + functions] += lax.fori_loop(0, count // width // unroll, body, zero)
 
@@ -238,9 +257,10 @@
                 t_hop(1 - side, j)().wait_recv()
                 at = side * half_rows + j * step
 
-                @pl.loop(0, shells)
-                def _(b):
-                    spread_nb[b] = jnp.dot(t_nb[b, at:at + step, :], picked(side, b),
+                blocks = jnp.dot(widen[...], jnp.concatenate([t_nb[side, j, b] for b in range(shells)], axis=1),
+                                 preferred_element_type=jnp.float32).astype(jnp.bfloat16)
+                for b in range(shells):
+                    spread_nb[b] = jnp.dot(blocks[:, b * span:(b + 1) * span], pick[side, b * span:(b + 1) * span, :],
                                            preferred_element_type=jnp.float32).astype(jnp.bfloat16)
                 contract(spread_nb, at, step, 0, 2 * functions if side == 0 else 0)
     flips[0] = tiles[:, 2 * functions:].T
@@ -301,7 +321,7 @@
         when(cond, make, lambda d: d.wait_send())
 
 
-def shards(chunks, three_index, coefficients, shell_size, ket_shell, ket_count):
+def shards(three_index, coefficients, shell_size, ket_shell, ket_count):
     shells, aux_rows, width, span = three_index.shape
     slots = span // width
     n_pair, n_aux, n_occ = (lax.axis_size(a) for a in ("pair", "aux", "occ"))
@@ -309,10 +329,11 @@
     orbitals = coefficients.shape[1]
     functions = shells * width
     rows = aux_rows * width // n_occ
-    kept = n_pair * shells * (width * 5 // 8)
-    nbas = -(-kept // 128) * 128
+    thin = shells * (width * 5 // 8)
+    nbas = -(-n_pair * thin // 128) * 128
+    chunks = rows // 2 // functions
     out_rows = functions // n_red
-    step = rows // 2 // chunks
+    step = functions
     bf16, f32 = jnp.bfloat16, jnp.float32
     dma = pltpu.SemaphoreType.DMA
     vmem = pl.BlockSpec(memory_space=pltpu.VMEM)
@@ -327,10 +348,13 @@
             pltpu.SMEM((shells, slots), jnp.int32),
             pltpu.SMEM((shells,), jnp.int32),
             pltpu.VMEM((shells, rows, span), bf16),
-            pltpu.VMEM((shells, rows, span), bf16),
+            pltpu.VMEM((2, chunks, shells, thin, span), bf16),
             pltpu.VMEM((nbas, n_occ * orbitals), bf16),
             pltpu.VMEM((3, shells * span, nbas), bf16),
-            pltpu.VMEM((2, nbas, nbas), bf16),
+            pltpu.VMEM((thin, functions), bf16),
+            pltpu.VMEM((functions, thin), bf16),
+            pltpu.VMEM((2, chunks, shells, thin, span), bf16),
+            pltpu.VMEM((nbas, 2 * nbas), bf16),
             pltpu.VMEM((shells, 2 * span, nbas), bf16),
             pltpu.VMEM((shells, rows, nbas), bf16),
             pltpu.VMEM((shells, rows, nbas), bf16),
@@ -363,7 +387,7 @@
 
 def solution(mesh):
     return jax.shard_map(
-        functools.partial(shards, 2),
+        shards,
         mesh=mesh,
         in_specs=(
             P(("parts", "pair"), "aux", None, None),

time: 46.4 us -> 31.6 us (0.68)
  Pallas kernels: 44.8 us -> 29.9 us
    pallas_call x1, Pallas kernels: 44.8 us -> 29.9 us  [shards(): pl.pallas_call(functools.partial(kernel, (n_pair, n_aux, n_occ, width, sl...]
where the time goes in v3:
time: 31.6 us; the launch traced here: 31.3 us
  Pallas kernels  29.9 us (95%)
  local copies, waits for them, and re-layouts  1.42 us (4%)
    pallas_call x1, Pallas kernels, shards(): pl.pallas_call(functools.partial(kernel, (n_pair, n_aux, n_occ, width, sl...  29.9 us
    unnamed x1, local copies, waits for them, and re-layouts  1.42 us

profile of v3, /device:TPU:0, one launch (start us, length us, event | category | flops | bytes accessed | tf_op | source)
XLA Modules:
  0.0 31.3 jit_solution(15638516731866455592)
XLA Ops:
  0.0 29.9 %shard_map.55 = f32[32,384]{1,0:T(8,128)} custom-call(bf16[8,1024,128]{2,1,0:T(8,128)(2,1)} %bitcast.1, bf16[128,512]{1,0:T(8,128)(2,1)} %coef_hbm.1, s32[8]{0:T(128)} %size_hbm.1, s32[8,8]{1,0:T(8,128)} %ket_hbm.1, s32[8]{0:T(128)} %cnt_hbm.1), custom_call_target="tpu_custom_call" | custom-call | tf_op jit(solution)/shard_map/pallas_call | solution.py:340
  29.9 1.4 %copy.7 = f32[32,384]{1,0:T(8,128)} copy(f32[32,384]{1,0:T(8,128)} %shard_map.55) | data formatting | bytes 98304

commit v4 on v3

--- a/solution.py
+++ b/solution.py
@@ -189,6 +189,14 @@
             scatter(2, 0, shells // 2)
         if s == 1 or n_pair == 2:
             scatter(2, shells // 2, shells)
+            for side, (has, way) in enumerate(sides):
+                @pl.when(has)
+                def _():
+                    info_hop(1 - side)().wait_recv()
+                    move = pltpu.make_async_copy(info_in.at[side], info_s.at[side], local_sem.at[1 + side])
+                    move.start()
+                    move.wait()
+                    select(side, lambda b, s: info_s[side, b, s], lambda b: info_s[side, b, slots])
     for delta in range(1, n_occ):
         arrive(across_in(z, 0, n_pair - 1, delta))
     for s in range(n_pair - 1):
@@ -242,14 +250,6 @@
         tiles[:, col:col + functions] += lax.fori_loop(0, count // width // unroll, body, zero)
 
     contract(spread, 0, rows, 0, functions)
-    for side, (has, way) in enumerate(sides):
-        @pl.when(has)
-        def _():
-            info_hop(1 - side)().wait_recv()
-            move = pltpu.make_async_copy(info_in.at[side], info_s.at[side], local_sem.at[1 + side])
-            move.start()
-            move.wait()
-            select(side, lambda b, s: info_s[side, b, s], lambda b: info_s[side, b, slots])
     for j in range(chunks):
         for side, (has, way) in enumerate(sides):
             @pl.when(has)

time: 31.6 us -> 30.8 us (0.975)
  Pallas kernels: 29.9 us -> 29.2 us
    pallas_call x1, Pallas kernels: 29.9 us -> 29.2 us  [shards(): pl.pallas_call(functools.partial(kernel, (n_pair, n_aux, n_occ, width, sl...]
where the time goes in v4:
time: 30.8 us; the launch traced here: 30.6 us
  Pallas kernels  29.2 us (95%)
  local copies, waits for them, and re-layouts  1.42 us (5%)
    pallas_call x1, Pallas kernels, shards(): pl.pallas_call(functools.partial(kernel, (n_pair, n_aux, n_occ, width, sl...  29.2 us
    unnamed x1, local copies, waits for them, and re-layouts  1.42 us

profile of v4, /device:TPU:0, one launch (start us, length us, event | category | flops | bytes accessed | tf_op | source)
XLA Modules:
  0.0 30.6 jit_solution(1609640239686181738)
XLA Ops:
  0.0 29.2 %shard_map.55 = f32[32,384]{1,0:T(8,128)} custom-call(bf16[8,1024,128]{2,1,0:T(8,128)(2,1)} %bitcast.1, bf16[128,512]{1,0:T(8,128)(2,1)} %coef_hbm.1, s32[8]{0:T(128)} %size_hbm.1, s32[8,8]{1,0:T(8,128)} %ket_hbm.1, s32[8]{0:T(128)} %cnt_hbm.1), custom_call_target="tpu_custom_call" | custom-call | tf_op jit(solution)/shard_map/pallas_call | solution.py:340
  29.2 1.4 %copy.7 = f32[32,384]{1,0:T(8,128)} copy(f32[32,384]{1,0:T(8,128)} %shard_map.55) | data formatting | bytes 98304
